TPU v7x, 32 devices: a whole 2x2x4 slice. The times are simulated.
32 devices in a mesh: tm: 4 (over y, x), space: 8 (over z, core).
Axes of the slice: x: 2, y: 2, z: 4, core: 2. Of those that a mesh axis runs over, the one named last changes fastest.
Arguments:
- start_values: float32 [4, 64, 128, 128], P('tm', 'space'), may hold values from -6 to 6
- regions: int32 [64, 128, 128], P('space'), may hold values from 0 to 3
- resistivity: float32 [4], replicated, may hold values from 0.1 to 1
Outputs:
- slice_ends: float32 [4, 64, 128, 128], P('tm', 'space')
All inputs are finite; a program needn't handle non-finite values.
Results may differ from a plain program's by a relative error of at most 0.0003.
Values sent between devices are 32-bit elements; how exact they have to be, the bound alone decides.
A program may use at most 64 MiB of HBM per device.

v0:
```python
import jax
import jax.numpy as jnp
from jax import lax
from jax.sharding import PartitionSpec as P

STEPS = 8


fine_step = 0.008


def padded(block, sides, width):
    for axis, dim in sides:
        count = lax.axis_size(axis)
        forward = [(i, i + 1) for i in range(count - 1)]
        backward = [(target, source) for source, target in forward]
        low = lax.ppermute(
            lax.slice_in_dim(block, block.shape[dim] - width, None, axis=dim), axis, forward
        )
        high = lax.ppermute(lax.slice_in_dim(block, 0, width, axis=dim), axis, backward)
        block = jnp.concatenate([low, block, high], axis=dim)
    return block


def passed_along(value, axis, steps):
    count = lax.axis_size(axis)
    initial, last = (max(0, -steps), min(count, count - steps))
    return lax.ppermute(value, axis, [(source, source + steps) for source in range(initial, last)])


def lookup(regions, resistivity):
    result = jnp.zeros(regions.shape, jnp.float32)
    for region in range(resistivity.shape[0]):
        result = result + jnp.where(regions == region, resistivity[region], jnp.float32(0.0))
    return result


def conduct(field_pad, resist_pad, step_size):
    squared = field_pad * field_pad
    coeff = resist_pad * (1.0 + squared / (1.0 + squared))
    center = field_pad[1:-1, 1:-1, 1:-1]
    coeff_mid = coeff[1:-1, 1:-1, 1:-1]
    flux_sum = jnp.zeros_like(center)
    for axis_dim in range(3):
        for offset in (0, 2):
            index_list = [slice(1, -1)] * 3
            index_list[axis_dim] = slice(offset, offset + center.shape[axis_dim])
            neighbor = field_pad[tuple(index_list)]
            neighbor_coeff = coeff[tuple(index_list)]
            flux_sum = flux_sum + 0.5 * (coeff_mid + neighbor_coeff) * (neighbor - center)
    return center + step_size * flux_sum


def pad_slab(field):
    return jnp.pad(field, ((0, 0), (1, 1), (1, 1)))


def per_device(start_values, regions, resistivity):
    resist = lookup(regions, resistivity)
    coarse_step = fine_step * STEPS
    start = start_values[0]
    local_rows = start.shape[0]
    depth = 4
    total_rows = local_rows * lax.axis_size("space")
    resist_deep = pad_slab(padded(resist, (("space", 0),), depth))
    field = start
    guess = None
    for block in range(STEPS // depth):
        current = padded(field, (("space", 0),), depth)
        if block == 0:
            guess = conduct(
                pad_slab(current[depth - 1 : depth + local_rows + 1]),
                resist_deep[depth - 1 : depth + local_rows + 1],
                coarse_step,
            )
        for inner in range(depth):
            span = current.shape[0]
            stepped = conduct(pad_slab(current), resist_deep[inner : inner + span], fine_step)
            first_row = lax.axis_index("space") * local_rows - depth + inner + 1
            global_rows = first_row + jnp.arange(span - 2, dtype=jnp.int32)
            inside = (global_rows >= 0) & (global_rows < total_rows)
            current = jnp.where(inside[:, None, None], stepped, jnp.float32(0.0))
        field = current
    resist_pad = resist_deep[depth - 1 : depth + local_rows + 1]
    first = lax.axis_index("tm") == 0
    sent = jnp.where(first, field, field - guess)

    def relay_turn(turn, carry):
        incoming = passed_along(carry, "tm", 1)
        incoming_rim = padded(incoming, (("space", 0),), 1)
        advanced = conduct(pad_slab(incoming_rim), resist_pad, coarse_step) + sent
        return jnp.where(first, sent, advanced)

    result = lax.fori_loop(0, lax.axis_size("tm") - 1, relay_turn, sent)
    return result[None]


def solution(mesh):
    in_specs = (P("tm", "space", None, None), P("space", None, None), P())
    out_specs = P("tm", "space", None, None)
    return jax.shard_map(
        per_device, mesh=mesh, in_specs=in_specs, out_specs=out_specs, check_vma=False
    )
```

profile of v0, /device:TPU:12, one launch (start us, length us, event | category | flops | bytes accessed | tf_op | source)
XLA Modules:
  0.0 138.6 jit_solution(11187420633199300155)
XLA Ops:
  1.5 3.8 %select_add_fusion = f32[8,128,128]{2,1,0:T(8,128)S(1)} fusion(s32[8,128,128]{2,1,0:T(8,128)} %param.6, f32[]{:T(128)} %bitcast.6, f32[]{:T(128)} %bitcast.5, f32[]{:T(128)} %bitcast.4, f32[]{:T(128)} %bitcast.3), kind=kLoop, calls=%fused_computation.419 | loop fusion | flops 1441792 | bytes 1048592 | tf_op jit(solution)/shard_map/add | solution.py:34
  7.3 3.6 %collective-permute-start.6 = (f32[4,128,128]{2,1,0:T(8,128)S(1)}, f32[4,128,128]{2,1,0:T(8,128)}, u32[]{:S(2)}, u32[]{:S(2)}) collective-permute-start(f32[4,128,128]{2,1,0:T(8,128)S(1)} %get-tuple-element.93), channel_id=1, source_target_pairs={{1,0},{2,1},{3,2},{4,3},{5,4},{6,5},{7,6},{9,8},{10,9},{11,10},{12... | collective-permute-start | bytes 786440 | tf_op jit(solution)/shard_map/ppermute | solution.py:20
  12.9 3.6 %collective-permute-start.4 = (f32[4,128,128]{2,1,0:T(8,128)S(1)}, f32[4,128,128]{2,1,0:T(8,128)S(1)}, u32[]{:S(2)}, u32[]{:S(2)}) collective-permute-start(f32[4,128,128]{2,1,0:T(8,128)S(1)} %get-tuple-element.95), channel_id=1, source_target_pairs={{1,0},{2,1},{3,2},{4,3},{5,4},{6,5},{7,6},{9,8},{10,9},{11,10},{12... | collective-permute-start | bytes 786440 | tf_op jit(solution)/shard_map/ppermute | solution.py:20
  21.8 2.3 %select_maximum_fusion.2 = (f32[16,130,130]{2,1,0:T(8,128)S(1)}, f32[16,130,130]{2,1,0:T(8,128)S(1)}) fusion(f32[4,128,128]{2,1,0:T(8,128)} %collective-permute-done.6, f32[8,128,128]{2,1,0:T(8,128)S(1)} %select_add_fusion, f32[4,128,128]{2,1,0:T(8,128)} %copy-done.5, f32[16,128,128]{2,1,0:T(8,128)S(1)} %pad_maximum_fusion.2), kind=kLoop, calls=%fused_computation.105 | loop fusion | flops 5408000 | bytes 4260352 | tf_op jit(solution)/shard_map/concatenate | solution.py:21
  24.1 2.2 %fusion.55 = f32[14,128,128]{2,1,0:T(8,128)S(1)} fusion(f32[16,128,128]{2,1,0:T(8,128)S(1)} %pad_maximum_fusion.2, f32[16,130,130]{2,1,0:T(8,128)S(1)} %get-tuple-element.89, pred[14]{0:T(512)(128)(4,1)S(1)} %compare_and_fusion), kind=kLoop, calls=%fused_computation.137 | loop fusion | flops 7340032 | bytes 11141632 | tf_op jit(solution)/shard_map/jit(_where)/select_n | solution.py:82
  30.6 2.3 %fusion.265 = (f32[10,130,130]{2,1,0:T(8,128)}, f32[10,130,130]{2,1,0:T(8,128)}, f32[10,130,130]{2,1,0:T(8,128)S(1)}) fusion(f32[16,130,130]{2,1,0:T(8,128)S(1)} %get-tuple-element.88, f32[10,128,128]{2,1,0:T(8,128)S(1)} %slice.798, f32[10,128,128]{2,1,0:T(8,128)S(1)} %fusion.151), kind=kLoop, calls=%fused_computation.427 | loop fusion | flops 1690000 | bytes 4014720 | tf_op jit(solution)/shard_map/slice | solution.py:78
  35.8 3.8 %collective-permute-start.7 = (f32[4,128,128]{2,1,0:T(8,128)}, f32[4,128,128]{2,1,0:T(8,128)}, u32[]{:S(2)}, u32[]{:S(2)}) collective-permute-start(f32[4,128,128]{2,1,0:T(8,128)} %get-tuple-element.90), channel_id=1, source_target_pairs={{0,1},{1,2},{2,3},{3,4},{4,5},{5,6},{6,7},{8,9},{9,10},{10,11},{11... | collective-permute-start | bytes 786440 | tf_op jit(solution)/shard_map/ppermute | solution.py:17
  39.5 2.2 %collective-permute-start.8 = (f32[4,128,128]{2,1,0:T(8,128)}, f32[4,128,128]{2,1,0:T(8,128)}, u32[]{:S(2)}, u32[]{:S(2)}) collective-permute-start(f32[4,128,128]{2,1,0:T(8,128)} %get-tuple-element.91), channel_id=1, source_target_pairs={{1,0},{2,1},{3,2},{4,3},{5,4},{6,5},{7,6},{9,8},{10,9},{11,10},{12... | collective-permute-start | bytes 786440 | tf_op jit(solution)/shard_map/ppermute | solution.py:20
  41.7 2.2 %collective-permute-done.7 = f32[4,128,128]{2,1,0:T(8,128)} collective-permute-done((f32[4,128,128]{2,1,0:T(8,128)}, f32[4,128,128]{2,1,0:T(8,128)}, u32[]{:S(2)}, u32[]{:S(2)}) %collective-permute-start.7) | collective-permute-done | bytes 262176 | tf_op jit(solution)/shard_map/ppermute | solution.py:17
  47.0 2.2 %fusion.29 = f32[16,130,130]{2,1,0:T(8,128)S(1)} fusion(f32[16,128,128]{2,1,0:T(8,128)S(1)} %pad_maximum_fusion.3, f32[4,128,128]{2,1,0:T(8,128)} %collective-permute-done.6, f32[8,128,128]{2,1,0:T(8,128)S(1)} %select_add_fusion, f32[4,128,128]{2,1,0:T(8,128)S(1)} %copy-done.6), kind=kLoop, calls=%fused_computation.104 | loop fusion | flops 5408000 | bytes 3178752 | tf_op jit(solution)/shard_map/mul | solution.py:40
  49.1 2.2 %fusion.70 = f32[14,128,128]{2,1,0:T(8,128)S(1)} fusion(f32[16,128,128]{2,1,0:T(8,128)S(1)} %pad_maximum_fusion.3, f32[16,130,130]{2,1,0:T(8,128)S(1)} %fusion.29, pred[14]{0:T(512)(128)(4,1)S(1)} %compare_and_fusion), kind=kLoop, calls=%fused_computation.152 | loop fusion | flops 7340032 | bytes 11141632 | tf_op jit(solution)/shard_map/jit(_where)/select_n | solution.py:82
  57.3 2.7 %subtract_select_fusion = f32[8,128,128]{2,1,0:T(8,128)S(1)} fusion(f32[10,128,128]{2,1,0:T(8,128)S(1)} %fusion.166, f32[8,128,128]{2,1,0:T(8,128)S(1)} %bitcast.11, f32[10,128,128]{2,1,0:T(8,128)S(1)} %slice.798, f32[10,130,130]{2,1,0:T(8,128)S(1)} %copy-done.1, f32[4,128,128]{2,1,0:T(8,128)S(1)} %copy-done.10, f32[4,128,128]{2,1,0:T(8,128)S(1)} %copy-done.8, ...), kind=kLoop, calls=%fused_computation.257 | loop fusion | flops 8781824 | bytes 11796993 | tf_op jit(solution)/shard_map/jit(_where)/select_n | solution.py:86
  60.1 77.6 %while.12 = (s32[]{:T(128)}, f32[8,128,128]{2,1,0:T(8,128)S(1)}, pred[]{:T(512)}, f32[10,130,130]{2,1,0:T(8,128)S(1)}, f32[8,128,128]{2,1,0:T(8,128)S(1)}, /*index=5*/s32[]{:T(128)}) while((s32[]{:T(128)}, f32[8,128,128]{2,1,0:T(8,128)S(1)}, pred[]{:T(512)}, f32[10,130,130]{2,1,0:T(8,128)S(1)}, f32[8,128,128]{2,1,0:T(8,128)S(1)}, ...), condition=%wide.region_1.2_spmd, body=%wide.region_0.1_spmd.sunk | while | flops 7967522 | bytes 13038238 | solution.py:94
  60.1 3.4 %collective-permute-start = (f32[8,128,128]{2,1,0:T(8,128)S(1)}, f32[8,128,128]{2,1,0:T(8,128)S(1)}, u32[]{:S(2)}, u32[]{:S(2)}) collective-permute-start(f32[8,128,128]{2,1,0:T(8,128)S(1)} %get-tuple-element.146), channel_id=1, source_target_pairs={{0,8},{8,16},{16,24},{1,9},{9,17},{17,25},{2,10},{10,18},{18,26},{... | collective-permute-start | bytes 1572872 | tf_op jit(solution)/shard_map/while/body/eval_jaxpr/ppermute | solution.py:28
  63.5 13.3 %collective-permute-done = f32[8,128,128]{2,1,0:T(8,128)S(1)} collective-permute-done((f32[8,128,128]{2,1,0:T(8,128)S(1)}, f32[8,128,128]{2,1,0:T(8,128)S(1)}, u32[]{:S(2)}, u32[]{:S(2)}) %collective-permute-start) | collective-permute-done | bytes 524320 | tf_op jit(solution)/shard_map/while/body/eval_jaxpr/ppermute | solution.py:28
  78.8 2.6 %collective-permute-start.2 = (f32[1,128,128]{2,1,0:T(8,128)S(1)}, f32[1,128,128]{2,1,0:T(8,128)S(1)}, u32[]{:S(2)}, u32[]{:S(2)}) collective-permute-start(f32[1,128,128]{2,1,0:T(8,128)S(1)} %get-tuple-element.136), channel_id=1, source_target_pairs={{0,1},{1,2},{2,3},{3,4},{4,5},{5,6},{6,7},{8,9},{9,10},{10,11},{11... | collective-permute-start | bytes 196616 | tf_op jit(solution)/shard_map/while/body/eval_jaxpr/ppermute | solution.py:17
  81.4 3.0 %collective-permute-done.2 = f32[1,128,128]{2,1,0:T(8,128)S(1)} collective-permute-done((f32[1,128,128]{2,1,0:T(8,128)S(1)}, f32[1,128,128]{2,1,0:T(8,128)S(1)}, u32[]{:S(2)}, u32[]{:S(2)}) %collective-permute-start.2) | collective-permute-done | bytes 65568 | tf_op jit(solution)/shard_map/while/body/eval_jaxpr/ppermute | solution.py:17
  86.3 2.5 %collective-permute-start = (f32[8,128,128]{2,1,0:T(8,128)S(1)}, f32[8,128,128]{2,1,0:T(8,128)S(1)}, u32[]{:S(2)}, u32[]{:S(2)}) collective-permute-start(f32[8,128,128]{2,1,0:T(8,128)S(1)} %get-tuple-element.146), channel_id=1, source_target_pairs={{0,8},{8,16},{16,24},{1,9},{9,17},{17,25},{2,10},{10,18},{18,26},{... | collective-permute-start | bytes 1572872 | tf_op jit(solution)/shard_map/while/body/eval_jaxpr/ppermute | solution.py:28
  88.8 14.2 %collective-permute-done = f32[8,128,128]{2,1,0:T(8,128)S(1)} collective-permute-done((f32[8,128,128]{2,1,0:T(8,128)S(1)}, f32[8,128,128]{2,1,0:T(8,128)S(1)}, u32[]{:S(2)}, u32[]{:S(2)}) %collective-permute-start) | collective-permute-done | bytes 524320 | tf_op jit(solution)/shard_map/while/body/eval_jaxpr/ppermute | solution.py:28
  104.9 2.4 %collective-permute-start.2 = (f32[1,128,128]{2,1,0:T(8,128)S(1)}, f32[1,128,128]{2,1,0:T(8,128)S(1)}, u32[]{:S(2)}, u32[]{:S(2)}) collective-permute-start(f32[1,128,128]{2,1,0:T(8,128)S(1)} %get-tuple-element.136), channel_id=1, source_target_pairs={{0,1},{1,2},{2,3},{3,4},{4,5},{5,6},{6,7},{8,9},{9,10},{10,11},{11... | collective-permute-start | bytes 196616 | tf_op jit(solution)/shard_map/while/body/eval_jaxpr/ppermute | solution.py:17
  107.3 3.2 %collective-permute-done.2 = f32[1,128,128]{2,1,0:T(8,128)S(1)} collective-permute-done((f32[1,128,128]{2,1,0:T(8,128)S(1)}, f32[1,128,128]{2,1,0:T(8,128)S(1)}, u32[]{:S(2)}, u32[]{:S(2)}) %collective-permute-start.2) | collective-permute-done | bytes 65568 | tf_op jit(solution)/shard_map/while/body/eval_jaxpr/ppermute | solution.py:17
  114.3 14.0 %collective-permute-done = f32[8,128,128]{2,1,0:T(8,128)S(1)} collective-permute-done((f32[8,128,128]{2,1,0:T(8,128)S(1)}, f32[8,128,128]{2,1,0:T(8,128)S(1)}, u32[]{:S(2)}, u32[]{:S(2)}) %collective-permute-start) | collective-permute-done | bytes 524320 | tf_op jit(solution)/shard_map/while/body/eval_jaxpr/ppermute | solution.py:28
  130.3 2.4 %collective-permute-start.2 = (f32[1,128,128]{2,1,0:T(8,128)S(1)}, f32[1,128,128]{2,1,0:T(8,128)S(1)}, u32[]{:S(2)}, u32[]{:S(2)}) collective-permute-start(f32[1,128,128]{2,1,0:T(8,128)S(1)} %get-tuple-element.136), channel_id=1, source_target_pairs={{0,1},{1,2},{2,3},{3,4},{4,5},{5,6},{6,7},{8,9},{9,10},{10,11},{11... | collective-permute-start | bytes 196616 | tf_op jit(solution)/shard_map/while/body/eval_jaxpr/ppermute | solution.py:17
  132.7 3.2 %collective-permute-done.2 = f32[1,128,128]{2,1,0:T(8,128)S(1)} collective-permute-done((f32[1,128,128]{2,1,0:T(8,128)S(1)}, f32[1,128,128]{2,1,0:T(8,128)S(1)}, u32[]{:S(2)}, u32[]{:S(2)}) %collective-permute-start.2) | collective-permute-done | bytes 65568 | tf_op jit(solution)/shard_map/while/body/eval_jaxpr/ppermute | solution.py:17
  (69 shorter events, 40.7 us)
Async XLA Ops:
  0.0 10.9 %copy-start.2 = (f32[1,8,128,128]{3,2,1,0:T(8,128)S(1)}, f32[1,8,128,128]{3,2,1,0:T(8,128)}, u32[]{:S(2)}) copy-start(f32[1,8,128,128]{3,2,1,0:T(8,128)} %param.5) | copy-start | bytes 1572868
  5.3 15.2 %collective-permute-start.5 = (f32[4,128,128]{2,1,0:T(8,128)S(1)}, f32[4,128,128]{2,1,0:T(8,128)S(1)}, u32[]{:S(2)}, u32[]{:S(2)}) collective-permute-start(f32[4,128,128]{2,1,0:T(8,128)S(1)} %get-tuple-element.92), channel_id=1, source_target_pairs={{0,1},{1,2},{2,3},{3,4},{4,5},{5,6},{6,7},{8,9},{9,10},{10,11},{11... | collective-permute-start | bytes 786440 | tf_op jit(solution)/shard_map/ppermute | solution.py:17
  7.3 14.5 %collective-permute-start.6 = (f32[4,128,128]{2,1,0:T(8,128)S(1)}, f32[4,128,128]{2,1,0:T(8,128)}, u32[]{:S(2)}, u32[]{:S(2)}) collective-permute-start(f32[4,128,128]{2,1,0:T(8,128)S(1)} %get-tuple-element.93), channel_id=1, source_target_pairs={{1,0},{2,1},{3,2},{4,3},{5,4},{6,5},{7,6},{9,8},{10,9},{11,10},{12... | collective-permute-start | bytes 786440 | tf_op jit(solution)/shard_map/ppermute | solution.py:20
  11.0 7.7 %collective-permute-start.3 = (f32[4,128,128]{2,1,0:T(8,128)S(1)}, f32[4,128,128]{2,1,0:T(8,128)S(1)}, u32[]{:S(2)}, u32[]{:S(2)}) collective-permute-start(f32[4,128,128]{2,1,0:T(8,128)S(1)} %get-tuple-element.94), channel_id=1, source_target_pairs={{0,1},{1,2},{2,3},{3,4},{4,5},{5,6},{6,7},{8,9},{9,10},{10,11},{11... | collective-permute-start | bytes 786440 | tf_op jit(solution)/shard_map/ppermute | solution.py:17
  12.9 7.5 %collective-permute-start.4 = (f32[4,128,128]{2,1,0:T(8,128)S(1)}, f32[4,128,128]{2,1,0:T(8,128)S(1)}, u32[]{:S(2)}, u32[]{:S(2)}) collective-permute-start(f32[4,128,128]{2,1,0:T(8,128)S(1)} %get-tuple-element.95), channel_id=1, source_target_pairs={{1,0},{2,1},{3,2},{4,3},{5,4},{6,5},{7,6},{9,8},{10,9},{11,10},{12... | collective-permute-start | bytes 786440 | tf_op jit(solution)/shard_map/ppermute | solution.py:20
  18.7 1.9 %copy-start.7 = (f32[4,128,128]{2,1,0:T(8,128)}, f32[4,128,128]{2,1,0:T(8,128)S(1)}, u32[]{:S(2)}) copy-start(f32[4,128,128]{2,1,0:T(8,128)S(1)} %collective-permute-done.3) | copy-start | bytes 786436
  34.1 0.8 copy-start.4
  35.8 8.2 %collective-permute-start.7 = (f32[4,128,128]{2,1,0:T(8,128)}, f32[4,128,128]{2,1,0:T(8,128)}, u32[]{:S(2)}, u32[]{:S(2)}) collective-permute-start(f32[4,128,128]{2,1,0:T(8,128)} %get-tuple-element.90), channel_id=1, source_target_pairs={{0,1},{1,2},{2,3},{3,4},{4,5},{5,6},{6,7},{8,9},{9,10},{10,11},{11... | collective-permute-start | bytes 786440 | tf_op jit(solution)/shard_map/ppermute | solution.py:17
  39.5 6.2 %collective-permute-start.8 = (f32[4,128,128]{2,1,0:T(8,128)}, f32[4,128,128]{2,1,0:T(8,128)}, u32[]{:S(2)}, u32[]{:S(2)}) collective-permute-start(f32[4,128,128]{2,1,0:T(8,128)} %get-tuple-element.91), channel_id=1, source_target_pairs={{1,0},{2,1},{3,2},{4,3},{5,4},{6,5},{7,6},{9,8},{10,9},{11,10},{12... | collective-permute-start | bytes 786440 | tf_op jit(solution)/shard_map/ppermute | solution.py:20
  41.7 5.3 %copy-start.6 = (f32[4,128,128]{2,1,0:T(8,128)S(1)}, f32[4,128,128]{2,1,0:T(8,128)}, u32[]{:S(2)}) copy-start(f32[4,128,128]{2,1,0:T(8,128)} %copy-done.5) | copy-start | bytes 786436
  55.7 1.3 copy-start.1
  55.7 1.5 %copy-start.3 = (f32[1,8,128,128]{3,2,1,0:T(8,128)S(1)}, f32[1,8,128,128]{3,2,1,0:T(8,128)}, u32[]{:S(2)}) copy-start(f32[1,8,128,128]{3,2,1,0:T(8,128)} %param.5) | copy-start | bytes 1572868
  55.7 1.5 %copy-start.8 = (f32[4,128,128]{2,1,0:T(8,128)S(1)}, f32[4,128,128]{2,1,0:T(8,128)}, u32[]{:S(2)}) copy-start(f32[4,128,128]{2,1,0:T(8,128)} %copy-done.7) | copy-start | bytes 786436
  55.7 1.6 %copy-start.10 = (f32[4,128,128]{2,1,0:T(8,128)S(1)}, f32[4,128,128]{2,1,0:T(8,128)}, u32[]{:S(2)}) copy-start(f32[4,128,128]{2,1,0:T(8,128)} %copy-done.9) | copy-start | bytes 786436
  57.3 2.8 %copy-start = (f32[10,130,130]{2,1,0:T(8,128)S(1)}, f32[10,130,130]{2,1,0:T(8,128)}, u32[]{:S(2)}) copy-start(f32[10,130,130]{2,1,0:T(8,128)} %get-tuple-element.142) | copy-start | bytes 2028004
  60.1 16.7 %collective-permute-start = (f32[8,128,128]{2,1,0:T(8,128)S(1)}, f32[8,128,128]{2,1,0:T(8,128)S(1)}, u32[]{:S(2)}, u32[]{:S(2)}) collective-permute-start(f32[8,128,128]{2,1,0:T(8,128)S(1)} %get-tuple-element.146), channel_id=1, source_target_pairs={{0,8},{8,16},{16,24},{1,9},{9,17},{17,25},{2,10},{10,18},{18,26},{... | collective-permute-start | bytes 1572872 | tf_op jit(solution)/shard_map/while/body/eval_jaxpr/ppermute | solution.py:28
  76.9 4.5 %collective-permute-start.1 = (f32[1,128,128]{2,1,0:T(8,128)S(1)}, f32[1,128,128]{2,1,0:T(8,128)S(1)}, u32[]{:S(2)}, u32[]{:S(2)}) collective-permute-start(f32[1,128,128]{2,1,0:T(8,128)S(1)} %get-tuple-element.135), channel_id=1, source_target_pairs={{1,0},{2,1},{3,2},{4,3},{5,4},{6,5},{7,6},{9,8},{10,9},{11,10},{12... | collective-permute-start | bytes 196616 | tf_op jit(solution)/shard_map/while/body/eval_jaxpr/ppermute | solution.py:20
  78.8 5.6 %collective-permute-start.2 = (f32[1,128,128]{2,1,0:T(8,128)S(1)}, f32[1,128,128]{2,1,0:T(8,128)S(1)}, u32[]{:S(2)}, u32[]{:S(2)}) collective-permute-start(f32[1,128,128]{2,1,0:T(8,128)S(1)} %get-tuple-element.136), channel_id=1, source_target_pairs={{0,1},{1,2},{2,3},{3,4},{4,5},{5,6},{6,7},{8,9},{9,10},{10,11},{11... | collective-permute-start | bytes 196616 | tf_op jit(solution)/shard_map/while/body/eval_jaxpr/ppermute | solution.py:17
  86.3 16.7 %collective-permute-start = (f32[8,128,128]{2,1,0:T(8,128)S(1)}, f32[8,128,128]{2,1,0:T(8,128)S(1)}, u32[]{:S(2)}, u32[]{:S(2)}) collective-permute-start(f32[8,128,128]{2,1,0:T(8,128)S(1)} %get-tuple-element.146), channel_id=1, source_target_pairs={{0,8},{8,16},{16,24},{1,9},{9,17},{17,25},{2,10},{10,18},{18,26},{... | collective-permute-start | bytes 1572872 | tf_op jit(solution)/shard_map/while/body/eval_jaxpr/ppermute | solution.py:28
  103.0 4.3 %collective-permute-start.1 = (f32[1,128,128]{2,1,0:T(8,128)S(1)}, f32[1,128,128]{2,1,0:T(8,128)S(1)}, u32[]{:S(2)}, u32[]{:S(2)}) collective-permute-start(f32[1,128,128]{2,1,0:T(8,128)S(1)} %get-tuple-element.135), channel_id=1, source_target_pairs={{1,0},{2,1},{3,2},{4,3},{5,4},{6,5},{7,6},{9,8},{10,9},{11,10},{12... | collective-permute-start | bytes 196616 | tf_op jit(solution)/shard_map/while/body/eval_jaxpr/ppermute | solution.py:20
  104.9 5.6 %collective-permute-start.2 = (f32[1,128,128]{2,1,0:T(8,128)S(1)}, f32[1,128,128]{2,1,0:T(8,128)S(1)}, u32[]{:S(2)}, u32[]{:S(2)}) collective-permute-start(f32[1,128,128]{2,1,0:T(8,128)S(1)} %get-tuple-element.136), channel_id=1, source_target_pairs={{0,1},{1,2},{2,3},{3,4},{4,5},{5,6},{6,7},{8,9},{9,10},{10,11},{11... | collective-permute-start | bytes 196616 | tf_op jit(solution)/shard_map/while/body/eval_jaxpr/ppermute | solution.py:17
  112.4 16.0 %collective-permute-start = (f32[8,128,128]{2,1,0:T(8,128)S(1)}, f32[8,128,128]{2,1,0:T(8,128)S(1)}, u32[]{:S(2)}, u32[]{:S(2)}) collective-permute-start(f32[8,128,128]{2,1,0:T(8,128)S(1)} %get-tuple-element.146), channel_id=1, source_target_pairs={{0,8},{8,16},{16,24},{1,9},{9,17},{17,25},{2,10},{10,18},{18,26},{... | collective-permute-start | bytes 1572872 | tf_op jit(solution)/shard_map/while/body/eval_jaxpr/ppermute | solution.py:28
  128.3 4.3 %collective-permute-start.1 = (f32[1,128,128]{2,1,0:T(8,128)S(1)}, f32[1,128,128]{2,1,0:T(8,128)S(1)}, u32[]{:S(2)}, u32[]{:S(2)}) collective-permute-start(f32[1,128,128]{2,1,0:T(8,128)S(1)} %get-tuple-element.135), channel_id=1, source_target_pairs={{1,0},{2,1},{3,2},{4,3},{5,4},{6,5},{7,6},{9,8},{10,9},{11,10},{12... | collective-permute-start | bytes 196616 | tf_op jit(solution)/shard_map/while/body/eval_jaxpr/ppermute | solution.py:20
  130.3 5.6 %collective-permute-start.2 = (f32[1,128,128]{2,1,0:T(8,128)S(1)}, f32[1,128,128]{2,1,0:T(8,128)S(1)}, u32[]{:S(2)}, u32[]{:S(2)}) collective-permute-start(f32[1,128,128]{2,1,0:T(8,128)S(1)} %get-tuple-element.136), channel_id=1, source_target_pairs={{0,1},{1,2},{2,3},{3,4},{4,5},{5,6},{6,7},{8,9},{9,10},{10,11},{11... | collective-permute-start | bytes 196616 | tf_op jit(solution)/shard_map/while/body/eval_jaxpr/ppermute | solution.py:17
  (3 other events, 2.2 us)
where the time goes:
time: 139 us
  waiting for transfers between devices  58.6 us (42%)
  starting transfers between devices  38 us (27%)
  other arithmetic  34.9 us (25%)
  local copies, waits for them, and re-layouts  6.43 us (5%)
    ppermute x3, waiting for transfers between devices, passed_along(): lax.ppermute(value, axis, [(source, source + steps) for source in range(i...  41.5 us
    ppermute x6, starting transfers between devices, padded(): lax.ppermute(lax.slice_in_dim(block, 0, width, axis=dim), axis, backward)  15.2 us
    ppermute x6, starting transfers between devices, padded(): lax.ppermute(lax.slice_in_dim(block, block.shape[dim] - width, None, axis...  15 us
    ppermute x6, waiting for transfers between devices, padded(): lax.ppermute(lax.slice_in_dim(block, block.shape[dim] - width, None, axis...  13.6 us
    select_n x7, other arithmetic, per_device(): current = jnp.where(inside[:, None, None], stepped, jnp.float32(0.0))  12 us
    ppermute x3, starting transfers between devices, passed_along(): lax.ppermute(value, axis, [(source, source + steps) for source in range(i...  7.82 us
    mul x9, other arithmetic, conduct(): coeff = resist_pad * (1.0 + squared / (1.0 + squared))  6.53 us
    unnamed x25, local copies, waits for them, and re-layouts  3.97 us
  transfers between devices with their start and end apart: 15, of which 10 were waited for; matrix products, arithmetic and copies ran while one was open for 0% of the time, Pallas kernels for 0%

commit v1 on v0

v1 whole, which is shorter than its diff:
```python
import functools

import jax
import jax.numpy as jnp
from jax import lax
from jax.experimental import pallas as pl
from jax.experimental.pallas import tpu as pltpu
from jax.sharding import PartitionSpec as P

STEPS = 8
fine_step = 0.008
WIDTH = 2
PAD = 8
CHUNK = 32
STRIP = 16
MESH = pl.DeviceIdType.MESH


def coefficient(field, scaled):
    denominator = 1.0 + field * field
    estimate = pl.reciprocal(denominator, approx=True)
    inverse = estimate * (2.0 - denominator * estimate)
    return scaled * (2.0 - inverse)


def sweep(field_at, coeff_at, planes, row, count, emit):
    rows = pl.ds(row, count)
    lane = lax.broadcasted_iota(jnp.int32, (count, field_at.shape[-1]), 1)
    lanes = field_at.shape[-1]
    is_first, is_last = lane == 0, lane == lanes - 1
    low = planes.start
    before, here = field_at[low - 1, rows, :], field_at[low, rows, :]
    k_before, k_here = coeff_at[low - 1, rows, :], coeff_at[low, rows, :]
    flux_before = (k_before + k_here) * (here - before)
    for plane in planes:
        after, k_after = field_at[plane + 1, rows, :], coeff_at[plane + 1, rows, :]
        flux = (k_here + k_after) * (after - here)
        total = flux - flux_before
        for shift in (-1, 1):
            near = pl.ds(row + shift, count)
            total += (k_here + coeff_at[plane, near, :]) * (field_at[plane, near, :] - here)
        right = jnp.where(is_last, 0.0, pltpu.roll(here, lanes - 1, 1))
        k_right = jnp.where(is_last, 0.0, pltpu.roll(k_here, lanes - 1, 1))
        across = (k_here + k_right) * (right - here)
        total += across - jnp.where(is_first, k_here * here, pltpu.roll(across, 1, 1))
        emit(plane, here, total)
        here, k_here, flux_before = after, k_after, flux


def kernel(
    slices, blocks, start, regions, resistivity, out,
    field, coeff, scaled, halo, guess, relay, relay_coeff,
    halo_send, halo_recv, scaled_send, scaled_recv, relay_send, relay_recv, rim_send, rim_recv,
):
    count, height, lanes = start.shape
    low, high = WIDTH, WIDTH + count
    me_t, me_s = lax.axis_index("tm"), lax.axis_index("space")
    has_low, has_high = me_s > 0, me_s < blocks - 1
    has_prev, has_next = me_t > 0, me_t < slices - 1
    below, above = (me_t, me_s - 1), (me_t, me_s + 1)
    previous, following = (me_t - 1, me_s), (me_t + 1, me_s)
    sides = ((0, has_low, below), (1, has_high, above))

    def chunks(body, size=CHUNK):
        def turn(index, _):
            body(pl.multiple_of(index * size, size))
            return 0

        lax.fori_loop(0, height // size, turn, 0)

    for buffer in (field.at[0], field.at[1], coeff.at[0], coeff.at[1], relay, relay_coeff):
        edge = jnp.zeros((buffer.shape[0], PAD, lanes), jnp.float32)
        buffer[:, pl.ds(0, PAD), :] = edge
        buffer[:, pl.ds(PAD + height, PAD), :] = edge
    for side, present, _ in sides:
        @pl.when(jnp.logical_not(present))
        def _():
            halo[:, side] = jnp.zeros((2, WIDTH, height, lanes), jnp.float32)
            scaled[pl.ds(high * side, WIDTH)] = jnp.zeros((WIDTH, height, lanes), jnp.float32)
            relay[(count + 1) * side, pl.ds(PAD, height), :] = jnp.zeros((height, lanes), jnp.float32)

    barrier = pltpu.get_barrier_semaphore()
    partners = ((has_low, below), (has_high, above), (has_prev, previous), (has_next, following))
    for present, target in partners:
        @pl.when(present)
        def _():
            pl.semaphore_signal(barrier, inc=1, device_id=target, device_id_type=MESH)
    pl.semaphore_wait(barrier, sum(jnp.where(present, 1, 0) for present, _ in partners))

    def remote(source, target, send_sem, recv_sem, device):
        return pltpu.make_async_remote_copy(
            src_ref=source, dst_ref=target, send_sem=send_sem, recv_sem=recv_sem,
            device_id=device, device_id_type=MESH,
        )

    def halo_copy(side, device, slot, source):
        return remote(
            source.at[pl.ds((count - WIDTH) * side, WIDTH)], halo.at[slot, 1 - side],
            halo_send.at[slot, side], halo_recv.at[slot, 1 - side], device,
        )

    def scaled_copy(side, device):
        return remote(
            scaled.at[pl.ds(low + (count - WIDTH) * side, WIDTH)],
            scaled.at[pl.ds(high * (1 - side), WIDTH)],
            scaled_send.at[side], scaled_recv.at[1 - side], device,
        )

    inner = field.at[0, pl.ds(low, count), pl.ds(PAD, height), :]

    for side, present, device in sides:
        @pl.when(present)
        def _():
            halo_copy(side, device, 0, start).start()

    def lookup(plane, rows):
        region = regions[plane, rows, :]
        value = jnp.zeros(region.shape, jnp.float32)
        for index in range(resistivity.shape[0]):
            value = jnp.where(region == index, resistivity[index] * (0.5 * fine_step), value)
        return value

    order = list(range(WIDTH)) + list(range(count - WIDTH, count))

    def outer_scaled(row):
        for plane in order:
            scaled[low + plane, pl.ds(row, CHUNK), :] = lookup(plane, pl.ds(row, CHUNK))

    chunks(outer_scaled)
    for side, present, device in sides:
        @pl.when(present)
        def _():
            scaled_copy(side, device).start()

    def prepare(row):
        rows, padded = pl.ds(row, CHUNK), pl.ds(row + PAD, CHUNK)
        for plane in range(count):
            value = start[plane, rows, :]
            if plane in order:
                factor = scaled[low + plane, rows, :]
            else:
                factor = lookup(plane, rows)
                scaled[low + plane, rows, :] = factor
            field[0, low + plane, padded, :] = value
            coeff[0, low + plane, padded, :] = coefficient(value, factor)

    chunks(prepare)

    coarse = jnp.float32(STEPS)
    subtract = jnp.where(has_prev, 1.0, 0.0).astype(jnp.float32)
    keep = (jnp.where(has_low, 1.0, 0.0).astype(jnp.float32), jnp.where(has_high, 1.0, 0.0).astype(jnp.float32))

    def fine(step, now, planes):
        later = 1 - now
        first, last = step == 0, step == STEPS - 1

        def body(row):
            def emit(plane, value, increment):
                rows, padded = pl.ds(row, CHUNK), pl.ds(row + PAD, CHUNK)
                own = low <= plane < high
                stepped = value + increment
                if first and own:
                    guess[plane - low, rows, :] = subtract * (value + coarse * increment)
                if last:
                    out[plane - low, rows, :] = stepped - guess[plane - low, rows, :]
                    return
                if not own:
                    stepped = stepped * keep[0 if plane < low else 1]
                field[later, plane, padded, :] = stepped
                coeff[later, plane, padded, :] = coefficient(stepped, scaled[plane, rows, :])

            sweep(field.at[now], coeff.at[now], planes, row + PAD, CHUNK, emit)

        chunks(body)

    rounds = STEPS // WIDTH
    for turn in range(rounds):
        slot = turn % 2
        source = start if turn == 0 else inner
        for inside in range(WIDTH):
            fine(turn * WIDTH + inside, inside % 2, range(low + inside + 1, high - inside - 1))
        for side, present, device in sides:
            @pl.when(present)
            def _():
                copy = halo_copy(side, device, slot, source)
                copy.wait_send()
                if turn == 0:
                    scaled_copy(side, device).wait_send()
                    scaled_copy(1 - side, device).wait_recv()
                halo_copy(1 - side, device, slot, source).wait_recv()

            def place(row, side=side):
                rows, padded = pl.ds(row, CHUNK), pl.ds(row + PAD, CHUNK)
                for plane in range(WIDTH):
                    at = high * side + plane
                    value = halo[slot, side, plane, rows, :]
                    field[0, at, padded, :] = value
                    coeff[0, at, padded, :] = coefficient(value, scaled[at, rows, :])

            chunks(place)
            for inside in range(WIDTH):
                reach = WIDTH - 1 - inside
                if side == 0:
                    planes = range(low - reach, low + inside + 1)
                else:
                    planes = range(high - inside - 1, high + reach)
                fine(turn * WIDTH + inside, inside % 2, planes)
            if turn < rounds - 1:
                @pl.when(present)
                def _():
                    halo_copy(side, device, 1 - slot, inner).start()

    strips = height // STRIP

    def strip_rows(strip, offset):
        return pl.ds(pl.multiple_of(strip * STRIP + offset, STRIP if offset % STRIP == 0 else 8), STRIP)

    def relay_copy(strip, device):
        return remote(
            out.at[:, strip_rows(strip, 0), :],
            relay.at[pl.ds(1, count), strip_rows(strip, PAD), :],
            relay_send.at[strip], relay_recv.at[strip], device,
        )

    def rim_copy(side, strip, device):
        rows = strip_rows(strip, PAD)
        return remote(
            relay.at[1 + (count - 1) * side, rows, :],
            relay.at[(count + 1) * (1 - side), rows, :],
            rim_send.at[side, strip], rim_recv.at[1 - side, strip], device,
        )

    @pl.when(jnp.logical_not(has_prev))
    def _():
        def send(strip, _):
            relay_copy(strip, following).start()
            return 0

        lax.fori_loop(0, strips, send, 0)

    @pl.when(has_prev)
    def _():
        def arrive(strip):
            relay_copy(strip, previous).wait_recv()
            for side, present, device in sides:
                @pl.when(present)
                def _():
                    rim_copy(side, strip, device).start()
            rows, padded = strip_rows(strip, 0), strip_rows(strip, PAD)
            for plane in range(count):
                relay_coeff[1 + plane, padded, :] = coefficient(
                    relay[1 + plane, padded, :], scaled[low + plane, rows, :]
                )

        def advance(strip):
            rows, padded = strip_rows(strip, 0), strip_rows(strip, PAD)
            for side, present, device in sides:
                @pl.when(present)
                def _():
                    rim_copy(1 - side, strip, device).wait_recv()
                at = (count + 1) * side
                relay_coeff[at, padded, :] = coefficient(
                    relay[at, padded, :], scaled[low - 1 + at, rows, :]
                )

            def emit(plane, value, increment):
                out[plane - 1, rows, :] = out[plane - 1, rows, :] + (value + coarse * increment)

            sweep(relay, relay_coeff, range(1, count + 1), padded.start, STRIP, emit)

            @pl.when(has_next)
            def _():
                relay_copy(strip, following).start()

        arrive(0)

        def turn(strip, _):
            arrive(strip)
            advance(strip - 1)
            return 0

        lax.fori_loop(1, strips, turn, 0)
        advance(strips - 1)

        def finish(strip, _):
            for side, present, device in sides:
                @pl.when(present)
                def _():
                    rim_copy(side, strip, device).wait_send()
            return 0

        lax.fori_loop(0, strips, finish, 0)

    @pl.when(has_next)
    def _():
        def finish(strip, _):
            relay_copy(strip, following).wait_send()
            return 0

        lax.fori_loop(0, strips, finish, 0)


def per_device(slices, blocks, start_values, regions, resistivity):
    start = start_values[0]
    count, height, lanes = start.shape
    tall, deep = height + 2 * PAD, count + 2 * WIDTH
    strips = height // STRIP
    dma, vmem = pltpu.SemaphoreType.DMA, pltpu.VMEM
    f32 = jnp.float32
    result = pl.pallas_call(
        functools.partial(kernel, slices, blocks),
        out_shape=jax.ShapeDtypeStruct(start.shape, f32),
        in_specs=[
            pl.BlockSpec(memory_space=pltpu.VMEM),
            pl.BlockSpec(memory_space=pltpu.VMEM),
            pl.BlockSpec(memory_space=pltpu.SMEM),
        ],
        out_specs=pl.BlockSpec(memory_space=pltpu.VMEM),
        scratch_shapes=[
            vmem((2, deep, tall, lanes), f32),
            vmem((2, deep, tall, lanes), f32),
            vmem((deep, height, lanes), f32),
            vmem((2, 2, WIDTH, height, lanes), f32),
            vmem(start.shape, f32),
            vmem((count + 2, tall, lanes), f32),
            vmem((count + 2, tall, lanes), f32),
            dma((2, 2)), dma((2, 2)), dma((2,)), dma((2,)),
            dma((strips,)), dma((strips,)), dma((2, strips)), dma((2, strips)),
        ],
        compiler_params=pltpu.CompilerParams(
            collective_id=0, has_side_effects=True, vmem_limit_bytes=32 * 2**20
        ),
        cost_estimate=pl.CostEstimate(flops=start.size * 400, bytes_accessed=start.size * 12, transcendentals=0),
    )(start, regions, resistivity)
    return result[None]


def solution(mesh):
    in_specs = (P("tm", "space", None, None), P("space", None, None), P())
    out_specs = P("tm", "space", None, None)
    return jax.shard_map(
        functools.partial(per_device, mesh.shape["tm"], mesh.shape["space"]),
        mesh=mesh, in_specs=in_specs, out_specs=out_specs, check_vma=False,
    )
```

time: 139 us -> 58.1 us (0.42)
  the two profiles are of different devices: /device:TPU:12 before, /device:TPU:15 now
where the time goes in v1:
time: 58.1 us; the launch traced here: 57.8 us
  Pallas kernels  54.3 us (93%)
  local copies, waits for them, and re-layouts  3.53 us (6%)
    pallas_call x1, Pallas kernels, per_device(): pl.pallas_call(functools.partial(kernel, slices, blocks), out_shape=jax.S...  54.3 us
    unnamed x7, local copies, waits for them, and re-layouts  3.53 us

profile of v1, /device:TPU:15, one launch (start us, length us, event | category | flops | bytes accessed | tf_op | source)
XLA Modules:
  0.0 57.8 jit_solution(12673923109162239615)
XLA Ops:
  0.0 0.0 copy-start.2
  0.0 0.7 %copy-done.2 = f32[4]{0:T(128)S(1)} copy-done((f32[4]{0:T(128)S(1)}, f32[4]{0:T(128)}, u32[]{:S(2)}) %copy-start.2) | copy-done | bytes 40
  0.7 0.0 copy-start
  0.7 1.0 %copy-done = f32[1,8,128,128]{3,2,1,0:T(8,128)S(1)} copy-done((f32[1,8,128,128]{3,2,1,0:T(8,128)S(1)}, f32[1,8,128,128]{3,2,1,0:T(8,128)}, u32[]{:S(2)}) %copy-start) | copy-done | bytes 524312
  1.7 0.0 copy-start.1
  1.7 1.0 %copy-done.1 = s32[8,128,128]{2,1,0:T(8,128)S(1)} copy-done((s32[8,128,128]{2,1,0:T(8,128)S(1)}, s32[8,128,128]{2,1,0:T(8,128)}, u32[]{:S(2)}) %copy-start.1) | copy-done | bytes 524312
  2.7 54.3 %shard_map.37 = f32[8,128,128]{2,1,0:T(8,128)S(1)} custom-call(f32[8,128,128]{2,1,0:T(8,128)S(1)} %bitcast.3, s32[8,128,128]{2,1,0:T(8,128)S(1)} %copy-done.1, f32[4]{0:T(128)S(1)} %copy-done.2), custom_call_target="tpu_custom_call" | custom-call | flops 52428800 | bytes 1572864 | tf_op jit(solution)/shard_map/pallas_call | solution.py:310
  57.0 0.8 %copy.5 = f32[1,8,128,128]{3,2,1,0:T(8,128)} copy(f32[1,8,128,128]{3,2,1,0:T(8,128)S(1)} %bitcast.2) | data formatting | bytes 1048576
Async XLA Ops:
  0.0 0.7 %copy-start.2 = (f32[4]{0:T(128)S(1)}, f32[4]{0:T(128)}, u32[]{:S(2)}) copy-start(f32[4]{0:T(128)} %resistivity.1) | copy-start | bytes 52
  0.7 1.0 %copy-start = (f32[1,8,128,128]{3,2,1,0:T(8,128)S(1)}, f32[1,8,128,128]{3,2,1,0:T(8,128)}, u32[]{:S(2)}) copy-start(f32[1,8,128,128]{3,2,1,0:T(8,128)} %param.3) | copy-start | bytes 1572868
  1.7 1.0 %copy-start.1 = (s32[8,128,128]{2,1,0:T(8,128)S(1)}, s32[8,128,128]{2,1,0:T(8,128)}, u32[]{:S(2)}) copy-start(s32[8,128,128]{2,1,0:T(8,128)} %regions.1) | copy-start | bytes 1572868

commit v2 on v1

--- a/solution.py
+++ b/solution.py
@@ -12,7 +12,9 @@
 WIDTH = 2
 PAD = 8
 CHUNK = 32
-STRIP = 16
+STRIP = 8
+LAG = 2
+HELD = 2
 MESH = pl.DeviceIdType.MESH
 
 
@@ -32,6 +34,7 @@
     before, here = field_at[low - 1, rows, :], field_at[low, rows, :]
     k_before, k_here = coeff_at[low - 1, rows, :], coeff_at[low, rows, :]
     flux_before = (k_before + k_here) * (here - before)
+    held = []
     for plane in planes:
         after, k_after = field_at[plane + 1, rows, :], coeff_at[plane + 1, rows, :]
         flux = (k_here + k_after) * (after - here)
@@ -43,16 +46,30 @@
         k_right = jnp.where(is_last, 0.0, pltpu.roll(k_here, lanes - 1, 1))
         across = (k_here + k_right) * (right - here)
         total += across - jnp.where(is_first, k_here * here, pltpu.roll(across, 1, 1))
-        emit(plane, here, total)
+        held.append(emit(plane, here, total))
+        if len(held) > HELD:
+            held.pop(0)()
         here, k_here, flux_before = after, k_after, flux
+    for store in held:
+        store()
 
 
 def kernel(
-    slices, blocks, start, regions, resistivity, out,
-    field, coeff, scaled, halo, guess, relay, relay_coeff,
+    slices, blocks, start_hbm, regions_hbm, resistivity_hbm, out,
+    start, regions, resistivity, field_even, field_odd, coeff_even, coeff_odd,
+    scaled, halo, guess, relay, relay_coeff, input_sem,
     halo_send, halo_recv, scaled_send, scaled_recv, relay_send, relay_recv, rim_send, rim_recv,
 ):
     count, height, lanes = start.shape
+    field, coeff = (field_even, field_odd), (coeff_even, coeff_odd)
+    inputs = [
+        pltpu.make_async_copy(source, target, input_sem.at[index])
+        for index, (source, target) in enumerate(
+            ((resistivity_hbm, resistivity), (regions_hbm, regions), (start_hbm, start))
+        )
+    ]
+    for copy in inputs:
+        copy.start()
     low, high = WIDTH, WIDTH + count
     me_t, me_s = lax.axis_index("tm"), lax.axis_index("space")
     has_low, has_high = me_s > 0, me_s < blocks - 1
@@ -68,7 +85,7 @@
 
         lax.fori_loop(0, height // size, turn, 0)
 
-    for buffer in (field.at[0], field.at[1], coeff.at[0], coeff.at[1], relay, relay_coeff):
+    for buffer in (*field, *coeff, relay, relay_coeff):
         edge = jnp.zeros((buffer.shape[0], PAD, lanes), jnp.float32)
         buffer[:, pl.ds(0, PAD), :] = edge
         buffer[:, pl.ds(PAD + height, PAD), :] = edge
@@ -106,12 +123,12 @@
             scaled_send.at[side], scaled_recv.at[1 - side], device,
         )
 
-    inner = field.at[0, pl.ds(low, count), pl.ds(PAD, height), :]
+    inner = field_even.at[pl.ds(low, count), pl.ds(PAD, height), :]
 
     for side, present, device in sides:
         @pl.when(present)
         def _():
-            halo_copy(side, device, 0, start).start()
+            halo_copy(side, device, 0, start_hbm).start()
 
     def lookup(plane, rows):
         region = regions[plane, rows, :]
@@ -126,6 +143,8 @@
         for plane in order:
             scaled[low + plane, pl.ds(row, CHUNK), :] = lookup(plane, pl.ds(row, CHUNK))
 
+    inputs[0].wait()
+    inputs[1].wait()
     chunks(outer_scaled)
     for side, present, device in sides:
         @pl.when(present)
@@ -141,9 +160,10 @@
             else:
                 factor = lookup(plane, rows)
                 scaled[low + plane, rows, :] = factor
-            field[0, low + plane, padded, :] = value
-            coeff[0, low + plane, padded, :] = coefficient(value, factor)
-
+            field_even[low + plane, padded, :] = value
+            coeff_even[low + plane, padded, :] = coefficient(value, factor)
+
+    inputs[2].wait()
     chunks(prepare)
 
     coarse = jnp.float32(STEPS)
@@ -159,24 +179,33 @@
                 rows, padded = pl.ds(row, CHUNK), pl.ds(row + PAD, CHUNK)
                 own = low <= plane < high
                 stepped = value + increment
-                if first and own:
-                    guess[plane - low, rows, :] = subtract * (value + coarse * increment)
                 if last:
-                    out[plane - low, rows, :] = stepped - guess[plane - low, rows, :]
-                    return
+                    result = stepped - guess[plane - low, rows, :]
+
+                    def store_last():
+                        out[plane - low, rows, :] = result
+
+                    return store_last
                 if not own:
                     stepped = stepped * keep[0 if plane < low else 1]
-                field[later, plane, padded, :] = stepped
-                coeff[later, plane, padded, :] = coefficient(stepped, scaled[plane, rows, :])
-
-            sweep(field.at[now], coeff.at[now], planes, row + PAD, CHUNK, emit)
+                factor = coefficient(stepped, scaled[plane, rows, :])
+
+                def store():
+                    if first and own:
+                        guess[plane - low, rows, :] = subtract * (value + coarse * increment)
+                    field[later][plane, padded, :] = stepped
+                    coeff[later][plane, padded, :] = factor
+
+                return store
+
+            sweep(field[now], coeff[now], planes, row + PAD, CHUNK, emit)
 
         chunks(body)
 
     rounds = STEPS // WIDTH
     for turn in range(rounds):
         slot = turn % 2
-        source = start if turn == 0 else inner
+        source = start_hbm if turn == 0 else inner
         for inside in range(WIDTH):
             fine(turn * WIDTH + inside, inside % 2, range(low + inside + 1, high - inside - 1))
         for side, present, device in sides:
@@ -194,8 +223,8 @@
                 for plane in range(WIDTH):
                     at = high * side + plane
                     value = halo[slot, side, plane, rows, :]
-                    field[0, at, padded, :] = value
-                    coeff[0, at, padded, :] = coefficient(value, scaled[at, rows, :])
+                    field_even[at, padded, :] = value
+                    coeff_even[at, padded, :] = coefficient(value, scaled[at, rows, :])
 
             chunks(place)
             for inside in range(WIDTH):
@@ -264,7 +293,12 @@
                 )
 
             def emit(plane, value, increment):
-                out[plane - 1, rows, :] = out[plane - 1, rows, :] + (value + coarse * increment)
+                result = out[plane - 1, rows, :] + (value + coarse * increment)
+
+                def store():
+                    out[plane - 1, rows, :] = result
+
+                return store
 
             sweep(relay, relay_coeff, range(1, count + 1), padded.start, STRIP, emit)
 
@@ -272,15 +306,17 @@
             def _():
                 relay_copy(strip, following).start()
 
-        arrive(0)
+        for strip in range(LAG):
+            arrive(strip)
 
         def turn(strip, _):
             arrive(strip)
-            advance(strip - 1)
-            return 0
-
-        lax.fori_loop(1, strips, turn, 0)
-        advance(strips - 1)
+            advance(strip - LAG)
+            return 0
+
+        lax.fori_loop(LAG, strips, turn, 0)
+        for strip in range(strips - LAG, strips):
+            advance(strip)
 
         def finish(strip, _):
             for side, present, device in sides:
@@ -311,20 +347,22 @@
         functools.partial(kernel, slices, blocks),
         out_shape=jax.ShapeDtypeStruct(start.shape, f32),
         in_specs=[
-            pl.BlockSpec(memory_space=pltpu.VMEM),
-            pl.BlockSpec(memory_space=pltpu.VMEM),
-            pl.BlockSpec(memory_space=pltpu.SMEM),
+            pl.BlockSpec(memory_space=pltpu.HBM),
+            pl.BlockSpec(memory_space=pltpu.HBM),
+            pl.BlockSpec(memory_space=pltpu.HBM),
         ],
         out_specs=pl.BlockSpec(memory_space=pltpu.VMEM),
         scratch_shapes=[
-            vmem((2, deep, tall, lanes), f32),
-            vmem((2, deep, tall, lanes), f32),
+            vmem(start.shape, f32),
+            vmem(regions.shape, regions.dtype),
+            pltpu.SMEM(resistivity.shape, f32),
+            *[vmem((deep, tall, lanes), f32) for _ in range(4)],
             vmem((deep, height, lanes), f32),
             vmem((2, 2, WIDTH, height, lanes), f32),
             vmem(start.shape, f32),
             vmem((count + 2, tall, lanes), f32),
             vmem((count + 2, tall, lanes), f32),
-            dma((2, 2)), dma((2, 2)), dma((2,)), dma((2,)),
+            dma((3,)), dma((2, 2)), dma((2, 2)), dma((2,)), dma((2,)),
             dma((strips,)), dma((strips,)), dma((2, strips)), dma((2, strips)),
         ],
         compiler_params=pltpu.CompilerParams(

time: 58.1 us -> 58.4 us (level)
  no operation moved by 1% of the time
where the time goes in v2:
time: 58.4 us; the launch traced here: 58 us
  Pallas kernels  54.4 us (93%)
  local copies, waits for them, and re-layouts  3.53 us (6%)
    pallas_call x1, Pallas kernels, per_device(): pl.pallas_call(functools.partial(kernel, slices, blocks), out_shape=jax.S...  54.4 us
    unnamed x7, local copies, waits for them, and re-layouts  3.53 us

profile of v2, /device:TPU:15, one launch (start us, length us, event | category | flops | bytes accessed | tf_op | source)
XLA Modules:
  0.0 58.0 jit_solution(12331617350156269262)
XLA Ops:
  0.0 0.0 copy-start.2
  0.0 0.7 %copy-done.2 = f32[4]{0:T(128)S(1)} copy-done((f32[4]{0:T(128)S(1)}, f32[4]{0:T(128)}, u32[]{:S(2)}) %copy-start.2) | copy-done | bytes 40
  0.7 0.0 copy-start
  0.7 1.0 %copy-done = f32[1,8,128,128]{3,2,1,0:T(8,128)S(1)} copy-done((f32[1,8,128,128]{3,2,1,0:T(8,128)S(1)}, f32[1,8,128,128]{3,2,1,0:T(8,128)}, u32[]{:S(2)}) %copy-start) | copy-done | bytes 524312
  1.7 0.0 copy-start.1
  1.7 1.0 %copy-done.1 = s32[8,128,128]{2,1,0:T(8,128)S(1)} copy-done((s32[8,128,128]{2,1,0:T(8,128)S(1)}, s32[8,128,128]{2,1,0:T(8,128)}, u32[]{:S(2)}) %copy-start.1) | copy-done | bytes 524312
  2.7 54.4 %shard_map.37 = f32[8,128,128]{2,1,0:T(8,128)S(1)} custom-call(f32[8,128,128]{2,1,0:T(8,128)S(1)} %bitcast.3, s32[8,128,128]{2,1,0:T(8,128)S(1)} %copy-done.1, f32[4]{0:T(128)S(1)} %copy-done.2), custom_call_target="tpu_custom_call" | custom-call | flops 52428800 | bytes 1572864 | tf_op jit(solution)/shard_map/pallas_call | solution.py:346
  57.2 0.8 %copy.5 = f32[1,8,128,128]{3,2,1,0:T(8,128)} copy(f32[1,8,128,128]{3,2,1,0:T(8,128)S(1)} %bitcast.2) | data formatting | bytes 1048576
Async XLA Ops:
  0.0 0.7 %copy-start.2 = (f32[4]{0:T(128)S(1)}, f32[4]{0:T(128)}, u32[]{:S(2)}) copy-start(f32[4]{0:T(128)} %resistivity_hbm.1) | copy-start | bytes 52
  0.7 1.0 %copy-start = (f32[1,8,128,128]{3,2,1,0:T(8,128)S(1)}, f32[1,8,128,128]{3,2,1,0:T(8,128)}, u32[]{:S(2)}) copy-start(f32[1,8,128,128]{3,2,1,0:T(8,128)} %param.3) | copy-start | bytes 1572868
  1.7 1.0 %copy-start.1 = (s32[8,128,128]{2,1,0:T(8,128)S(1)}, s32[8,128,128]{2,1,0:T(8,128)}, u32[]{:S(2)}) copy-start(s32[8,128,128]{2,1,0:T(8,128)} %regions_hbm.1) | copy-start | bytes 1572868

commit v3 on v2

--- a/solution.py
+++ b/solution.py
@@ -14,6 +14,7 @@
 CHUNK = 32
 STRIP = 8
 LAG = 2
+FLIGHT = 2
 HELD = 2
 MESH = pl.DeviceIdType.MESH
 
@@ -261,11 +262,17 @@
 
     @pl.when(jnp.logical_not(has_prev))
     def _():
+        for strip in range(FLIGHT):
+            relay_copy(strip, following).start()
+
         def send(strip, _):
+            relay_copy(strip - FLIGHT, following).wait_send()
             relay_copy(strip, following).start()
             return 0
 
-        lax.fori_loop(0, strips, send, 0)
+        lax.fori_loop(FLIGHT, strips, send, 0)
+        for strip in range(strips - FLIGHT, strips):
+            relay_copy(strip, following).wait_send()
 
     @pl.when(has_prev)
     def _():
@@ -327,7 +334,7 @@
 
         lax.fori_loop(0, strips, finish, 0)
 
-    @pl.when(has_next)
+    @pl.when(jnp.logical_and(has_prev, has_next))
     def _():
         def finish(strip, _):
             relay_copy(strip, following).wait_send()

time: 58.4 us -> 58.6 us (level)
  no operation moved by 1% of the time
where the time goes in v3:
time: 58.6 us; the launch traced here: 57.9 us
  Pallas kernels  54.4 us (93%)
  local copies, waits for them, and re-layouts  3.53 us (6%)
    pallas_call x1, Pallas kernels, per_device(): pl.pallas_call(functools.partial(kernel, slices, blocks), out_shape=jax.S...  54.4 us
    unnamed x7, local copies, waits for them, and re-layouts  3.53 us

profile of v3, /device:TPU:15, one launch (start us, length us, event | category | flops | bytes accessed | tf_op | source)
XLA Modules:
  0.0 57.9 jit_solution(17860651453048914768)
XLA Ops:
  0.0 0.0 copy-start.2
  0.0 0.7 %copy-done.2 = f32[4]{0:T(128)S(1)} copy-done((f32[4]{0:T(128)S(1)}, f32[4]{0:T(128)}, u32[]{:S(2)}) %copy-start.2) | copy-done | bytes 40
  0.7 0.0 copy-start
  0.7 1.0 %copy-done = f32[1,8,128,128]{3,2,1,0:T(8,128)S(1)} copy-done((f32[1,8,128,128]{3,2,1,0:T(8,128)S(1)}, f32[1,8,128,128]{3,2,1,0:T(8,128)}, u32[]{:S(2)}) %copy-start) | copy-done | bytes 524312
  1.7 0.0 copy-start.1
  1.7 1.0 %copy-done.1 = s32[8,128,128]{2,1,0:T(8,128)S(1)} copy-done((s32[8,128,128]{2,1,0:T(8,128)S(1)}, s32[8,128,128]{2,1,0:T(8,128)}, u32[]{:S(2)}) %copy-start.1) | copy-done | bytes 524312
  2.7 54.4 %shard_map.37 = f32[8,128,128]{2,1,0:T(8,128)S(1)} custom-call(f32[8,128,128]{2,1,0:T(8,128)S(1)} %bitcast.3, s32[8,128,128]{2,1,0:T(8,128)S(1)} %copy-done.1, f32[4]{0:T(128)S(1)} %copy-done.2), custom_call_target="tpu_custom_call" | custom-call | flops 52428800 | bytes 1572864 | tf_op jit(solution)/shard_map/pallas_call | solution.py:353
  57.2 0.8 %copy.5 = f32[1,8,128,128]{3,2,1,0:T(8,128)} copy(f32[1,8,128,128]{3,2,1,0:T(8,128)S(1)} %bitcast.2) | data formatting | bytes 1048576
Async XLA Ops:
  0.0 0.7 %copy-start.2 = (f32[4]{0:T(128)S(1)}, f32[4]{0:T(128)}, u32[]{:S(2)}) copy-start(f32[4]{0:T(128)} %resistivity_hbm.1) | copy-start | bytes 52
  0.7 1.0 %copy-start = (f32[1,8,128,128]{3,2,1,0:T(8,128)S(1)}, f32[1,8,128,128]{3,2,1,0:T(8,128)}, u32[]{:S(2)}) copy-start(f32[1,8,128,128]{3,2,1,0:T(8,128)} %param.3) | copy-start | bytes 1572868
  1.7 1.0 %copy-start.1 = (s32[8,128,128]{2,1,0:T(8,128)S(1)}, s32[8,128,128]{2,1,0:T(8,128)}, u32[]{:S(2)}) copy-start(s32[8,128,128]{2,1,0:T(8,128)} %regions_hbm.1) | copy-start | bytes 1572868

commit v4 on v3

--- a/solution.py
+++ b/solution.py
@@ -13,8 +13,8 @@
 PAD = 8
 CHUNK = 32
 STRIP = 8
-LAG = 2
-FLIGHT = 2
+LAG = 4
+FLIGHT = 4
 HELD = 2
 MESH = pl.DeviceIdType.MESH
 
@@ -204,12 +204,13 @@
         chunks(body)
 
     rounds = STEPS // WIDTH
+    is_even = lax.rem(me_s, 2) == 0
     for turn in range(rounds):
         slot = turn % 2
         source = start_hbm if turn == 0 else inner
         for inside in range(WIDTH):
             fine(turn * WIDTH + inside, inside % 2, range(low + inside + 1, high - inside - 1))
-        for side, present, device in sides:
+        def finish_side(side, present, device, turn=turn, slot=slot, source=source):
             @pl.when(present)
             def _():
                 copy = halo_copy(side, device, slot, source)
@@ -239,6 +240,16 @@
                 @pl.when(present)
                 def _():
                     halo_copy(side, device, 1 - slot, inner).start()
+
+        @pl.when(is_even)
+        def _():
+            for side in reversed(sides):
+                finish_side(*side)
+
+        @pl.when(jnp.logical_not(is_even))
+        def _():
+            for side in sides:
+                finish_side(*side)
 
     strips = height // STRIP
 
@@ -373,7 +384,7 @@
             dma((strips,)), dma((strips,)), dma((2, strips)), dma((2, strips)),
         ],
         compiler_params=pltpu.CompilerParams(
-            collective_id=0, has_side_effects=True, vmem_limit_bytes=32 * 2**20
+            collective_id=0, has_side_effects=True, vmem_limit_bytes=64 * 2**20
         ),
         cost_estimate=pl.CostEstimate(flops=start.size * 400, bytes_accessed=start.size * 12, transcendentals=0),
     )(start, regions, resistivity)

time: 58.6 us -> 55.6 us (0.949)
  local copies, waits for them, and re-layouts: 3.53 us -> 1.87 us
  Pallas kernels: 54.4 us -> 53.6 us
    unnamed x7 -> x1, local copies, waits for them, and re-layouts: 3.53 us -> 1.87 us
    pallas_call x1, Pallas kernels: 54.4 us -> 53.6 us  [per_device(): pl.pallas_call(functools.partial(kernel, slices, blocks), out_shape=jax.S...]
where the time goes in v4:
time: 55.6 us; the launch traced here: 55.4 us
  Pallas kernels  53.6 us (96%)
  local copies, waits for them, and re-layouts  1.87 us (3%)
    pallas_call x1, Pallas kernels, per_device(): pl.pallas_call(functools.partial(kernel, slices, blocks), out_shape=jax.S...  53.6 us
    unnamed x1, local copies, waits for them, and re-layouts  1.87 us

profile of v4, /device:TPU:15, one launch (start us, length us, event | category | flops | bytes accessed | tf_op | source)
XLA Modules:
  0.0 55.4 jit_solution(13171152445200000482)
XLA Ops:
  0.0 53.6 %shard_map.37 = f32[8,128,128]{2,1,0:T(8,128)} custom-call(f32[8,128,128]{2,1,0:T(8,128)} %bitcast.3, s32[8,128,128]{2,1,0:T(8,128)} %regions_hbm.1, f32[4]{0:T(128)} %resistivity_hbm.1), custom_call_target="tpu_custom_call" | custom-call | flops 52428800 | bytes 1572864 | tf_op jit(solution)/shard_map/pallas_call | solution.py:364
  53.6 1.9 %copy.5 = f32[1,8,128,128]{3,2,1,0:T(8,128)} copy(f32[1,8,128,128]{3,2,1,0:T(8,128)} %bitcast.2) | data formatting | bytes 1048576

commit v5 on v4

--- a/solution.py
+++ b/solution.py
@@ -9,12 +9,12 @@
 
 STEPS = 8
 fine_step = 0.008
-WIDTH = 2
+WIDTH = 4
 PAD = 8
 CHUNK = 32
 STRIP = 8
-LAG = 4
-FLIGHT = 4
+LAG = 1
+FLIGHT = 3
 HELD = 2
 MESH = pl.DeviceIdType.MESH
 
@@ -58,7 +58,7 @@
 def kernel(
     slices, blocks, start_hbm, regions_hbm, resistivity_hbm, out,
     start, regions, resistivity, field_even, field_odd, coeff_even, coeff_odd,
-    scaled, halo, guess, relay, relay_coeff, input_sem,
+    scaled, halo, outgoing, guess, relay, relay_coeff, input_sem,
     halo_send, halo_recv, scaled_send, scaled_recv, relay_send, relay_recv, rim_send, rim_recv,
 ):
     count, height, lanes = start.shape
@@ -98,7 +98,10 @@
             relay[(count + 1) * side, pl.ds(PAD, height), :] = jnp.zeros((height, lanes), jnp.float32)
 
     barrier = pltpu.get_barrier_semaphore()
-    partners = ((has_low, below), (has_high, above), (has_prev, previous), (has_next, following))
+    partners = [(has_low, below), (has_high, above), (has_prev, previous), (has_next, following)]
+    for in_time, step in ((has_prev, -1), (has_next, 1)):
+        for present, move in ((has_low, -1), (has_high, 1)):
+            partners.append((jnp.logical_and(in_time, present), (me_t + step, me_s + move)))
     for present, target in partners:
         @pl.when(present)
         def _():
@@ -123,8 +126,6 @@
             scaled.at[pl.ds(high * (1 - side), WIDTH)],
             scaled_send.at[side], scaled_recv.at[1 - side], device,
         )
-
-    inner = field_even.at[pl.ds(low, count), pl.ds(PAD, height), :]
 
     for side, present, device in sides:
         @pl.when(present)
@@ -172,6 +173,8 @@
     keep = (jnp.where(has_low, 1.0, 0.0).astype(jnp.float32), jnp.where(has_high, 1.0, 0.0).astype(jnp.float32))
 
     def fine(step, now, planes):
+        if not planes:
+            return
         later = 1 - now
         first, last = step == 0, step == STEPS - 1
 
@@ -194,6 +197,8 @@
                 def store():
                     if first and own:
                         guess[plane - low, rows, :] = subtract * (value + coarse * increment)
+                    if own and step % WIDTH == WIDTH - 1:
+                        outgoing[plane - low, rows, :] = stepped
                     field[later][plane, padded, :] = stepped
                     coeff[later][plane, padded, :] = factor
 
@@ -207,7 +212,7 @@
     is_even = lax.rem(me_s, 2) == 0
     for turn in range(rounds):
         slot = turn % 2
-        source = start_hbm if turn == 0 else inner
+        source = start_hbm if turn == 0 else outgoing
         for inside in range(WIDTH):
             fine(turn * WIDTH + inside, inside % 2, range(low + inside + 1, high - inside - 1))
         def finish_side(side, present, device, turn=turn, slot=slot, source=source):
@@ -239,7 +244,7 @@
             if turn < rounds - 1:
                 @pl.when(present)
                 def _():
-                    halo_copy(side, device, 1 - slot, inner).start()
+                    halo_copy(side, device, 1 - slot, outgoing).start()
 
         @pl.when(is_even)
         def _():
@@ -266,33 +271,43 @@
     def rim_copy(side, strip, device):
         rows = strip_rows(strip, PAD)
         return remote(
-            relay.at[1 + (count - 1) * side, rows, :],
+            out.at[(count - 1) * side, strip_rows(strip, 0), :],
             relay.at[(count + 1) * (1 - side), rows, :],
             rim_send.at[side, strip], rim_recv.at[1 - side, strip], device,
         )
+
+    def send_strip(strip):
+        for side, present, device in sides:
+            @pl.when(present)
+            def _():
+                rim_copy(side, strip, (device[0] + 1, device[1])).start()
+        relay_copy(strip, following).start()
+
+    def finish_strip(strip):
+        for side, present, device in sides:
+            @pl.when(present)
+            def _():
+                rim_copy(side, strip, (device[0] + 1, device[1])).wait_send()
+        relay_copy(strip, following).wait_send()
 
     @pl.when(jnp.logical_not(has_prev))
     def _():
         for strip in range(FLIGHT):
-            relay_copy(strip, following).start()
+            send_strip(strip)
 
         def send(strip, _):
-            relay_copy(strip - FLIGHT, following).wait_send()
-            relay_copy(strip, following).start()
+            finish_strip(strip - FLIGHT)
+            send_strip(strip)
             return 0
 
         lax.fori_loop(FLIGHT, strips, send, 0)
         for strip in range(strips - FLIGHT, strips):
-            relay_copy(strip, following).wait_send()
+            finish_strip(strip)
 
     @pl.when(has_prev)
     def _():
         def arrive(strip):
             relay_copy(strip, previous).wait_recv()
-            for side, present, device in sides:
-                @pl.when(present)
-                def _():
-                    rim_copy(side, strip, device).start()
             rows, padded = strip_rows(strip, 0), strip_rows(strip, PAD)
             for plane in range(count):
                 relay_coeff[1 + plane, padded, :] = coefficient(
@@ -322,7 +337,7 @@
 
             @pl.when(has_next)
             def _():
-                relay_copy(strip, following).start()
+                send_strip(strip)
 
         for strip in range(LAG):
             arrive(strip)
@@ -336,19 +351,10 @@
         for strip in range(strips - LAG, strips):
             advance(strip)
 
-        def finish(strip, _):
-            for side, present, device in sides:
-                @pl.when(present)
-                def _():
-                    rim_copy(side, strip, device).wait_send()
-            return 0
-
-        lax.fori_loop(0, strips, finish, 0)
-
     @pl.when(jnp.logical_and(has_prev, has_next))
     def _():
         def finish(strip, _):
-            relay_copy(strip, following).wait_send()
+            finish_strip(strip)
             return 0
 
         lax.fori_loop(0, strips, finish, 0)
@@ -378,6 +384,7 @@
             vmem((deep, height, lanes), f32),
             vmem((2, 2, WIDTH, height, lanes), f32),
             vmem(start.shape, f32),
+            vmem(start.shape, f32),
             vmem((count + 2, tall, lanes), f32),
             vmem((count + 2, tall, lanes), f32),
             dma((3,)), dma((2, 2)), dma((2, 2)), dma((2,)), dma((2,)),

time: 55.6 us -> 49.9 us (0.90)
  Pallas kernels: 53.6 us -> 47.4 us
    pallas_call x1, Pallas kernels: 53.6 us -> 47.4 us  [per_device(): pl.pallas_call(functools.partial(kernel, slices, blocks), out_shape=jax.S...]
where the time goes in v5:
time: 49.9 us; the launch traced here: 49.3 us
  Pallas kernels  47.4 us (95%)
  local copies, waits for them, and re-layouts  1.87 us (4%)
    pallas_call x1, Pallas kernels, per_device(): pl.pallas_call(functools.partial(kernel, slices, blocks), out_shape=jax.S...  47.4 us
    unnamed x1, local copies, waits for them, and re-layouts  1.87 us

profile of v5, /device:TPU:15, one launch (start us, length us, event | category | flops | bytes accessed | tf_op | source)
XLA Modules:
  0.0 49.3 jit_solution(17420077386961071219)
XLA Ops:
  0.0 47.4 %shard_map.37 = f32[8,128,128]{2,1,0:T(8,128)} custom-call(f32[8,128,128]{2,1,0:T(8,128)} %bitcast.3, s32[8,128,128]{2,1,0:T(8,128)} %regions_hbm.1, f32[4]{0:T(128)} %resistivity_hbm.1), custom_call_target="tpu_custom_call" | custom-call | flops 52428800 | bytes 1572864 | tf_op jit(solution)/shard_map/pallas_call | solution.py:370
  47.4 1.9 %copy.5 = f32[1,8,128,128]{3,2,1,0:T(8,128)} copy(f32[1,8,128,128]{3,2,1,0:T(8,128)} %bitcast.2) | data formatting | bytes 1048576

commit v6 on v5

--- a/solution.py
+++ b/solution.py
@@ -80,11 +80,8 @@
     sides = ((0, has_low, below), (1, has_high, above))
 
     def chunks(body, size=CHUNK):
-        def turn(index, _):
-            body(pl.multiple_of(index * size, size))
-            return 0
-
-        lax.fori_loop(0, height // size, turn, 0)
+        for index in range(height // size):
+            body(index * size)
 
     for buffer in (*field, *coeff, relay, relay_coeff):
         edge = jnp.zeros((buffer.shape[0], PAD, lanes), jnp.float32)

time: 49.9 us -> 54.2 us (1.086)
  Pallas kernels: 47.4 us -> 51.7 us
    pallas_call x1, Pallas kernels: 47.4 us -> 51.7 us  [per_device(): pl.pallas_call(functools.partial(kernel, slices, blocks), out_shape=jax.S...]
where the time goes in v6:
time: 54.2 us; the launch traced here: 53.6 us
  Pallas kernels  51.7 us (95%)
  local copies, waits for them, and re-layouts  1.87 us (3%)
    pallas_call x1, Pallas kernels, per_device(): pl.pallas_call(functools.partial(kernel, slices, blocks), out_shape=jax.S...  51.7 us
    unnamed x1, local copies, waits for them, and re-layouts  1.87 us

profile of v6, /device:TPU:15, one launch (start us, length us, event | category | flops | bytes accessed | tf_op | source)
XLA Modules:
  0.0 53.6 jit_solution(3040507395592119669)
XLA Ops:
  0.0 51.7 %shard_map.37 = f32[8,128,128]{2,1,0:T(8,128)} custom-call(f32[8,128,128]{2,1,0:T(8,128)} %bitcast.3, s32[8,128,128]{2,1,0:T(8,128)} %regions_hbm.1, f32[4]{0:T(128)} %resistivity_hbm.1), custom_call_target="tpu_custom_call" | custom-call | flops 52428800 | bytes 1572864 | tf_op jit(solution)/shard_map/pallas_call | solution.py:367
  51.7 1.9 %copy.5 = f32[1,8,128,128]{3,2,1,0:T(8,128)} copy(f32[1,8,128,128]{3,2,1,0:T(8,128)} %bitcast.2) | data formatting | bytes 1048576

commit v7 on v5

--- a/solution.py
+++ b/solution.py
@@ -26,17 +26,17 @@
     return scaled * (2.0 - inverse)
 
 
-def sweep(field_at, coeff_at, planes, row, count, emit):
+def sweep(field_at, coeff_at, low, number, row, count, emit):
     rows = pl.ds(row, count)
     lane = lax.broadcasted_iota(jnp.int32, (count, field_at.shape[-1]), 1)
     lanes = field_at.shape[-1]
     is_first, is_last = lane == 0, lane == lanes - 1
-    low = planes.start
     before, here = field_at[low - 1, rows, :], field_at[low, rows, :]
     k_before, k_here = coeff_at[low - 1, rows, :], coeff_at[low, rows, :]
     flux_before = (k_before + k_here) * (here - before)
     held = []
-    for plane in planes:
+    for position in range(number):
+        plane = low + position
         after, k_after = field_at[plane + 1, rows, :], coeff_at[plane + 1, rows, :]
         flux = (k_here + k_after) * (after - here)
         total = flux - flux_before
@@ -47,7 +47,7 @@
         k_right = jnp.where(is_last, 0.0, pltpu.roll(k_here, lanes - 1, 1))
         across = (k_here + k_right) * (right - here)
         total += across - jnp.where(is_first, k_here * here, pltpu.roll(across, 1, 1))
-        held.append(emit(plane, here, total))
+        held.append(emit(position, here, total))
         if len(held) > HELD:
             held.pop(0)()
         here, k_here, flux_before = after, k_after, flux
@@ -170,62 +170,69 @@
 
     coarse = jnp.float32(STEPS)
     subtract = jnp.where(has_prev, 1.0, 0.0).astype(jnp.float32)
-    keep = (jnp.where(has_low, 1.0, 0.0).astype(jnp.float32), jnp.where(has_high, 1.0, 0.0).astype(jnp.float32))
-
-    def fine(step, now, planes):
-        if not planes:
+
+    def fine(turn, inside, first, number, reach=0, side=None, present=None):
+        if number <= 0:
             return
-        later = 1 - now
-        first, last = step == 0, step == STEPS - 1
+        now, later = inside % 2, 1 - inside % 2
+        last = inside == WIDTH - 1
 
         def body(row):
-            def emit(plane, value, increment):
-                rows, padded = pl.ds(row, CHUNK), pl.ds(row + PAD, CHUNK)
-                own = low <= plane < high
+            rows, padded = pl.ds(row, CHUNK), pl.ds(row + PAD, CHUNK)
+
+            def emit(position, value, increment):
+                plane = first + position
                 stepped = value + increment
+                if reach:
+                    beyond = jnp.where(side == 0, position < reach, position > inside)
+                    grid = jnp.logical_or(present, jnp.logical_not(beyond))
+                    stepped = stepped * jnp.where(grid, 1.0, 0.0).astype(jnp.float32)
+                factor = coefficient(stepped, scaled[plane, rows, :])
+                if inside == 0:
+                    ahead = subtract * (value + coarse * increment)
+                    ahead = jnp.where(turn == 0, ahead, guess[plane, rows, :])
                 if last:
-                    result = stepped - guess[plane - low, rows, :]
-
-                    def store_last():
+                    result = stepped - guess[plane, rows, :]
+
+                def store():
+                    if inside == 0:
+                        guess[plane, rows, :] = ahead
+                    if last:
                         out[plane - low, rows, :] = result
-
-                    return store_last
-                if not own:
-                    stepped = stepped * keep[0 if plane < low else 1]
-                factor = coefficient(stepped, scaled[plane, rows, :])
-
-                def store():
-                    if first and own:
-                        guess[plane - low, rows, :] = subtract * (value + coarse * increment)
-                    if own and step % WIDTH == WIDTH - 1:
                         outgoing[plane - low, rows, :] = stepped
                     field[later][plane, padded, :] = stepped
                     coeff[later][plane, padded, :] = factor
 
                 return store
 
-            sweep(field[now], coeff[now], planes, row + PAD, CHUNK, emit)
+            sweep(field[now], coeff[now], first, number, row + PAD, CHUNK, emit)
 
         chunks(body)
 
     rounds = STEPS // WIDTH
     is_even = lax.rem(me_s, 2) == 0
-    for turn in range(rounds):
-        slot = turn % 2
-        source = start_hbm if turn == 0 else outgoing
+
+    def one_round(turn, _):
+        slot = lax.rem(turn, 2)
         for inside in range(WIDTH):
-            fine(turn * WIDTH + inside, inside % 2, range(low + inside + 1, high - inside - 1))
-        def finish_side(side, present, device, turn=turn, slot=slot, source=source):
+            fine(turn, inside, low + inside + 1, count - 2 * inside - 2)
+
+        def finish_side(index, _):
+            side = jnp.where(is_even, 1 - index, index)
+            present = jnp.where(side == 0, has_low, has_high)
+            device = (me_t, me_s + 2 * side - 1)
+
             @pl.when(present)
             def _():
-                copy = halo_copy(side, device, slot, source)
-                copy.wait_send()
-                if turn == 0:
-                    scaled_copy(side, device).wait_send()
-                    scaled_copy(1 - side, device).wait_recv()
-                halo_copy(1 - side, device, slot, source).wait_recv()
-
-            def place(row, side=side):
+                halo_copy(side, device, slot, outgoing).wait_send()
+                halo_copy(1 - side, device, slot, outgoing).wait_recv()
+
+            @pl.when(jnp.logical_and(present, turn == 0))
+            def _():
+                scaled_copy(side, device).wait_send()
+                scaled_copy(1 - side, device).wait_recv()
+
+            def place(row):
                 rows, padded = pl.ds(row, CHUNK), pl.ds(row + PAD, CHUNK)
                 for plane in range(WIDTH):
                     at = high * side + plane
@@ -236,25 +243,19 @@
             chunks(place)
             for inside in range(WIDTH):
                 reach = WIDTH - 1 - inside
-                if side == 0:
-                    planes = range(low - reach, low + inside + 1)
-                else:
-                    planes = range(high - inside - 1, high + reach)
-                fine(turn * WIDTH + inside, inside % 2, planes)
-            if turn < rounds - 1:
-                @pl.when(present)
-                def _():
-                    halo_copy(side, device, 1 - slot, outgoing).start()
-
-        @pl.when(is_even)
-        def _():
-            for side in reversed(sides):
-                finish_side(*side)
-
-        @pl.when(jnp.logical_not(is_even))
-        def _():
-            for side in sides:
-                finish_side(*side)
+                first = jnp.where(side == 0, low - reach, high - inside - 1)
+                fine(turn, inside, first, WIDTH, reach, side, present)
+
+            @pl.when(jnp.logical_and(present, turn < rounds - 1))
+            def _():
+                halo_copy(side, device, 1 - slot, outgoing).start()
+
+            return 0
+
+        lax.fori_loop(0, 2, finish_side, 0)
+        return 0
+
+    lax.fori_loop(0, rounds, one_round, 0)
 
     strips = height // STRIP
 
@@ -326,14 +327,14 @@
                 )
 
             def emit(plane, value, increment):
-                result = out[plane - 1, rows, :] + (value + coarse * increment)
+                result = out[plane, rows, :] + (value + coarse * increment)
 
                 def store():
-                    out[plane - 1, rows, :] = result
+                    out[plane, rows, :] = result
 
                 return store
 
-            sweep(relay, relay_coeff, range(1, count + 1), padded.start, STRIP, emit)
+            sweep(relay, relay_coeff, 1, count, padded.start, STRIP, emit)
 
             @pl.when(has_next)
             def _():
@@ -384,7 +385,7 @@
             vmem((deep, height, lanes), f32),
             vmem((2, 2, WIDTH, height, lanes), f32),
             vmem(start.shape, f32),
-            vmem(start.shape, f32),
+            vmem((deep, height, lanes), f32),
             vmem((count + 2, tall, lanes), f32),
             vmem((count + 2, tall, lanes), f32),
             dma((3,)), dma((2, 2)), dma((2, 2)), dma((2,)), dma((2,)),

time: 49.9 us -> 50.3 us (level)
  no operation moved by 1% of the time
where the time goes in v7:
time: 50.3 us; the launch traced here: 49.7 us
  Pallas kernels  47.8 us (95%)
  local copies, waits for them, and re-layouts  1.87 us (4%)
    pallas_call x1, Pallas kernels, per_device(): pl.pallas_call(functools.partial(kernel, slices, blocks), out_shape=jax.S...  47.8 us
    unnamed x1, local copies, waits for them, and re-layouts  1.87 us

profile of v7, /device:TPU:15, one launch (start us, length us, event | category | flops | bytes accessed | tf_op | source)
XLA Modules:
  0.0 49.7 jit_solution(15928056894979812908)
XLA Ops:
  0.0 47.8 %shard_map.37 = f32[8,128,128]{2,1,0:T(8,128)} custom-call(f32[8,128,128]{2,1,0:T(8,128)} %bitcast.3, s32[8,128,128]{2,1,0:T(8,128)} %regions_hbm.1, f32[4]{0:T(128)} %resistivity_hbm.1), custom_call_target="tpu_custom_call" | custom-call | flops 52428800 | bytes 1572864 | tf_op jit(solution)/shard_map/pallas_call | solution.py:371
  47.8 1.9 %copy.5 = f32[1,8,128,128]{3,2,1,0:T(8,128)} copy(f32[1,8,128,128]{3,2,1,0:T(8,128)} %bitcast.2) | data formatting | bytes 1048576

commit v8 on v7

--- a/solution.py
+++ b/solution.py
@@ -11,11 +11,11 @@
 fine_step = 0.008
 WIDTH = 4
 PAD = 8
-CHUNK = 32
+CHUNK = 64
 STRIP = 8
 LAG = 1
 FLIGHT = 3
-HELD = 2
+HELD = 1
 MESH = pl.DeviceIdType.MESH
 
 
@@ -86,6 +86,15 @@
 
         lax.fori_loop(0, height // size, turn, 0)
 
+    barrier = pltpu.get_barrier_semaphore()
+    partners = [(has_low, below), (has_high, above), (has_prev, previous), (has_next, following)]
+    for in_time, step in ((has_prev, -1), (has_next, 1)):
+        for present, move in ((has_low, -1), (has_high, 1)):
+            partners.append((jnp.logical_and(in_time, present), (me_t + step, me_s + move)))
+    for present, target in partners:
+        @pl.when(present)
+        def _():
+            pl.semaphore_signal(barrier, inc=1, device_id=target, device_id_type=MESH)
     for buffer in (*field, *coeff, relay, relay_coeff):
         edge = jnp.zeros((buffer.shape[0], PAD, lanes), jnp.float32)
         buffer[:, pl.ds(0, PAD), :] = edge
@@ -97,15 +106,6 @@
             scaled[pl.ds(high * side, WIDTH)] = jnp.zeros((WIDTH, height, lanes), jnp.float32)
             relay[(count + 1) * side, pl.ds(PAD, height), :] = jnp.zeros((height, lanes), jnp.float32)
 
-    barrier = pltpu.get_barrier_semaphore()
-    partners = [(has_low, below), (has_high, above), (has_prev, previous), (has_next, following)]
-    for in_time, step in ((has_prev, -1), (has_next, 1)):
-        for present, move in ((has_low, -1), (has_high, 1)):
-            partners.append((jnp.logical_and(in_time, present), (me_t + step, me_s + move)))
-    for present, target in partners:
-        @pl.when(present)
-        def _():
-            pl.semaphore_signal(barrier, inc=1, device_id=target, device_id_type=MESH)
     pl.semaphore_wait(barrier, sum(jnp.where(present, 1, 0) for present, _ in partners))
 
     def remote(source, target, send_sem, recv_sem, device):

time: 50.3 us -> 47.2 us (0.938)
  Pallas kernels: 47.8 us -> 44.9 us
    pallas_call x1, Pallas kernels: 47.8 us -> 44.9 us  [per_device(): pl.pallas_call(functools.partial(kernel, slices, blocks), out_shape=jax.S...]
where the time goes in v8:
time: 47.2 us; the launch traced here: 46.8 us
  Pallas kernels  44.9 us (95%)
  local copies, waits for them, and re-layouts  1.87 us (4%)
    pallas_call x1, Pallas kernels, per_device(): pl.pallas_call(functools.partial(kernel, slices, blocks), out_shape=jax.S...  44.9 us
    unnamed x1, local copies, waits for them, and re-layouts  1.87 us

profile of v8, /device:TPU:15, one launch (start us, length us, event | category | flops | bytes accessed | tf_op | source)
XLA Modules:
  0.0 46.8 jit_solution(13366259452283814797)
XLA Ops:
  0.0 44.9 %shard_map.37 = f32[8,128,128]{2,1,0:T(8,128)} custom-call(f32[8,128,128]{2,1,0:T(8,128)} %bitcast.3, s32[8,128,128]{2,1,0:T(8,128)} %regions_hbm.1, f32[4]{0:T(128)} %resistivity_hbm.1), custom_call_target="tpu_custom_call" | custom-call | flops 52428800 | bytes 1572864 | tf_op jit(solution)/shard_map/pallas_call | solution.py:371
  44.9 1.9 %copy.5 = f32[1,8,128,128]{3,2,1,0:T(8,128)} copy(f32[1,8,128,128]{3,2,1,0:T(8,128)} %bitcast.2) | data formatting | bytes 1048576

commit v9 on v8

--- a/solution.py
+++ b/solution.py
@@ -11,11 +11,11 @@
 fine_step = 0.008
 WIDTH = 4
 PAD = 8
-CHUNK = 64
+CHUNK = 128
 STRIP = 8
 LAG = 1
 FLIGHT = 3
-HELD = 1
+HELD = 0
 MESH = pl.DeviceIdType.MESH
 
 

time: 47.2 us -> 46.9 us (level)
  no operation moved by 1% of the time
where the time goes in v9:
time: 46.9 us; the launch traced here: 46.5 us
  Pallas kernels  44.7 us (95%)
  local copies, waits for them, and re-layouts  1.87 us (4%)
    pallas_call x1, Pallas kernels, per_device(): pl.pallas_call(functools.partial(kernel, slices, blocks), out_shape=jax.S...  44.7 us
    unnamed x1, local copies, waits for them, and re-layouts  1.87 us

profile of v9, /device:TPU:15, one launch (start us, length us, event | category | flops | bytes accessed | tf_op | source)
XLA Modules:
  0.0 46.5 jit_solution(2365120154135594645)
XLA Ops:
  0.0 44.7 %shard_map.37 = f32[8,128,128]{2,1,0:T(8,128)} custom-call(f32[8,128,128]{2,1,0:T(8,128)} %bitcast.3, s32[8,128,128]{2,1,0:T(8,128)} %regions_hbm.1, f32[4]{0:T(128)} %resistivity_hbm.1), custom_call_target="tpu_custom_call" | custom-call | flops 52428800 | bytes 1572864 | tf_op jit(solution)/shard_map/pallas_call | solution.py:371
  44.7 1.9 %copy.5 = f32[1,8,128,128]{3,2,1,0:T(8,128)} copy(f32[1,8,128,128]{3,2,1,0:T(8,128)} %bitcast.2) | data formatting | bytes 1048576

commit v10 on v9

--- a/solution.py
+++ b/solution.py
@@ -15,7 +15,6 @@
 STRIP = 8
 LAG = 1
 FLIGHT = 3
-HELD = 0
 MESH = pl.DeviceIdType.MESH
 
 
@@ -26,7 +25,7 @@
     return scaled * (2.0 - inverse)
 
 
-def sweep(field_at, coeff_at, low, number, row, count, emit):
+def sweep(field_at, coeff_at, low, number, row, count, emit, hold):
     rows = pl.ds(row, count)
     lane = lax.broadcasted_iota(jnp.int32, (count, field_at.shape[-1]), 1)
     lanes = field_at.shape[-1]
@@ -48,7 +47,7 @@
         across = (k_here + k_right) * (right - here)
         total += across - jnp.where(is_first, k_here * here, pltpu.roll(across, 1, 1))
         held.append(emit(position, here, total))
-        if len(held) > HELD:
+        if len(held) > hold:
             held.pop(0)()
         here, k_here, flux_before = after, k_after, flux
     for store in held:
@@ -205,7 +204,7 @@
 
                 return store
 
-            sweep(field[now], coeff[now], first, number, row + PAD, CHUNK, emit)
+            sweep(field[now], coeff[now], first, number, row + PAD, CHUNK, emit, 0)
 
         chunks(body)
 
@@ -334,7 +333,7 @@
 
                 return store
 
-            sweep(relay, relay_coeff, 1, count, padded.start, STRIP, emit)
+            sweep(relay, relay_coeff, 1, count, padded.start, STRIP, emit, count)
 
             @pl.when(has_next)
             def _():

time: 46.9 us -> 46.9 us (level)
  no operation moved by 1% of the time
where the time goes in v10:
time: 46.9 us; the launch traced here: 46.5 us
  Pallas kernels  44.7 us (95%)
  local copies, waits for them, and re-layouts  1.87 us (4%)
    pallas_call x1, Pallas kernels, per_device(): pl.pallas_call(functools.partial(kernel, slices, blocks), out_shape=jax.S...  44.7 us
    unnamed x1, local copies, waits for them, and re-layouts  1.87 us

profile of v10, /device:TPU:15, one launch (start us, length us, event | category | flops | bytes accessed | tf_op | source)
XLA Modules:
  0.0 46.5 jit_solution(2365120154135594645)
XLA Ops:
  0.0 44.7 %shard_map.37 = f32[8,128,128]{2,1,0:T(8,128)} custom-call(f32[8,128,128]{2,1,0:T(8,128)} %bitcast.3, s32[8,128,128]{2,1,0:T(8,128)} %regions_hbm.1, f32[4]{0:T(128)} %resistivity_hbm.1), custom_call_target="tpu_custom_call" | custom-call | flops 52428800 | bytes 1572864 | tf_op jit(solution)/shard_map/pallas_call | solution.py:370
  44.7 1.9 %copy.5 = f32[1,8,128,128]{3,2,1,0:T(8,128)} copy(f32[1,8,128,128]{3,2,1,0:T(8,128)} %bitcast.2) | data formatting | bytes 1048576
